TPU v7x, 32 devices: a whole 2x2x4 slice. The times are simulated.
32 devices in a mesh: scen: 2 (over y), rcv: 4 (over z), src: 2 (over x), tw: 2 (over core).
Axes of the slice: x: 2, y: 2, z: 4, core: 2. Of those that a mesh axis runs over, the one named last changes fastest.
Arguments:
- green_tiles: bfloat16 [256, 2, 2, 128, 128], P(('scen', 'rcv'), 'src', 'tw'), parts along dimension 0, may hold values from -0.1875 to 0.1875
- arrivals: int32 [256, 2, 2, 3], P('scen', 'src', 'tw'), parts along dimension 0, may hold values from 0 to 63, as said below
- counts: int32 [8, 2, 2, 4], P('scen', 'src', 'tw'), parts along dimension 0, may hold values from 0 to 16, as said below
- observed: bfloat16 [32, 1024, 128], P(('scen', 'rcv'), 'tw'), parts along dimension 0, may hold values from -6 to 6
- weights: float32 [32, 1024], P(('scen', 'rcv'), 'tw'), parts along dimension 0, may hold values from 0.25 to 4
- source_model: float32 [16384, 128], P(('scen', 'src')), parts along dimension 0, may hold values from -6 to 6
Outputs:
- model_update: float32 [4, 4096, 128], P(('scen', 'src'), ('rcv', 'tw')), parts along dimension 0
There are 2 independent parts, one for each index of `scen`. A program takes and returns all parts, laid end to end along the dimension named above; each array names one. Nothing has to cross between parts.
Inputs may be any that keep to these rules, and one draw needn't show every extreme that they name: `arrivals`: row h * 32 + t at source shard j and column k lists (gauge, source block, time block) of that holder's tile t; the gauge is one of 0 to 15, the source block one of j * 32 to j * 32 + 31 and the time block one of k * 4 to k * 4 + 3; a holder's tiles are listed in order of owner gauge // 4. counts[h, j, k, o] is the number of holder h's tiles in source shard j and column k whose owner is o; they sum to 32 over o; in each source shard and column some owner has exactly 16 tiles from every holder.
All inputs are finite; a program needn't handle non-finite values.
Results may differ from a plain program's by a relative error of at most 0.0027.
Values may be sent and summed in bfloat16 or wider, within the bound.
A program may use at most 64 MiB of HBM per device.

v0:
```python
import jax
import jax.numpy as jnp
from jax import lax
from jax.sharding import PartitionSpec as P

CG_ITERS = 2


damping = 0.5


def indicator(indices, length):
    return (indices[None, :] == jnp.arange(length, dtype=jnp.int32)[:, None]).astype(jnp.float32)


def select(values, indices):
    return jnp.take(values, jnp.maximum(indices, 0), axis=0)


def spread(indices, values, length):
    target = jnp.where(indices < 0, length, indices)
    return jax.ops.segment_sum(values, target, num_segments=length)


def squares_of(tile_block, weight_values):
    tile_wide = tile_block.astype(jnp.float32)
    return jnp.einsum(
        "ni,nij->nj", weight_values, tile_wide * tile_wide, precision=lax.Precision.HIGHEST
    )


def shards(green_tiles, arrivals, counts, observed, weights, source_model):
    own_tiles = green_tiles.reshape(
        green_tiles.shape[0], green_tiles.shape[3], green_tiles.shape[4]
    )
    tiles_dev, tile_rows, block_src = own_tiles.shape
    listing = arrivals.reshape(arrivals.shape[0], 3)
    owners = lax.axis_size("rcv")
    columns = lax.axis_size("tw")
    counts_all = counts.reshape(owners, owners)
    starts = jnp.cumsum(counts_all, axis=1) - counts_all
    gauges_dev, samples_dev, members = observed.shape
    blocks_col = samples_dev // tile_rows
    rows_dev = gauges_dev * blocks_col
    src_dev = source_model.shape[0]
    blocks_src = src_dev // block_src
    capacity = 2 * tiles_dev // owners
    owner_index = lax.axis_index("rcv")
    source_index = lax.axis_index("src")
    column_index = lax.axis_index("tw")
    slot_ids = jnp.arange(capacity, dtype=jnp.int32)
    holder_ids = jnp.arange(owners, dtype=jnp.int32)
    count_in = lax.dynamic_slice_in_dim(counts_all, owner_index, 1, 1)[:, 0]
    start_in = lax.dynamic_slice_in_dim(starts, owner_index, 1, 1)[:, 0]
    local_in = start_in[:, None] + slot_ids[None, :]
    valid_in = (slot_ids[None, :] < count_in[:, None]) & (local_in < tiles_dev)
    index_in = jnp.where(valid_in, holder_ids[:, None] * tiles_dev + local_in, 0).reshape(-1)
    listed_in = jnp.take(listing, index_in, axis=0)
    valid_in = valid_in.reshape(-1) & (listed_in[:, 0] // gauges_dev == owner_index)
    row_in = jnp.where(
        valid_in,
        (listed_in[:, 0] - owner_index * gauges_dev) * blocks_col
        + listed_in[:, 2]
        - column_index * blocks_col,
        -1,
    )
    block_in = jnp.where(valid_in, listed_in[:, 1] - source_index * blocks_src, -1)
    count_out = lax.dynamic_slice_in_dim(counts_all, owner_index, 1, 0)[0]
    start_out = lax.dynamic_slice_in_dim(starts, owner_index, 1, 0)[0]
    local_out = start_out[:, None] + slot_ids[None, :]
    valid_out = (slot_ids[None, :] < count_out[:, None]) & (local_out < tiles_dev)
    index_out = jnp.where(valid_out, local_out, 0).reshape(-1)
    listed_out = jnp.take(listing, owner_index * tiles_dev + index_out, axis=0)
    valid_out = valid_out.reshape(-1) & (
        listed_out[:, 0] // gauges_dev == jnp.repeat(holder_ids, capacity)
    )
    slot_tiles = jnp.where(
        valid_out[:, None, None],
        jnp.take(own_tiles, index_out, axis=0),
        jnp.zeros((), own_tiles.dtype),
    )
    held_tiles = lax.all_to_all(slot_tiles, "rcv", split_axis=0, concat_axis=0, tiled=True)
    block_table = indicator(block_in, blocks_src)

    def forward(coeffs):
        product = jnp.einsum(
            "nij,njk->nik", held_tiles, select(coeffs, block_in), preferred_element_type=jnp.float32
        )
        return spread(row_in, product, rows_dev)

    def adjoint(data_rows):
        product = jnp.einsum(
            "nij,nik->njk",
            held_tiles,
            select(data_rows, row_in),
            preferred_element_type=jnp.float32,
        )
        return spread(block_in, product, blocks_src)

    def settle(partial_rows):
        return (lax.psum(partial_rows, "src"), 0)

    def member_total(vector):
        return lax.psum(vector, ("rcv", "src", "tw"))

    model_half = source_model.astype(jnp.bfloat16).reshape(blocks_src, block_src, members)
    predicted, offset = settle(forward(model_half).reshape(gauges_dev, samples_dev, members))
    observed_piece = observed.astype(jnp.float32)
    misfit = observed_piece - predicted
    robust = weights[:, :, None] / (1.0 + misfit * misfit)
    adjoint_rows = (robust * misfit).astype(jnp.bfloat16).reshape(rows_dev, tile_rows, members)
    grad_part = adjoint(adjoint_rows).reshape(src_dev, members)
    diag_part = jnp.dot(
        block_table,
        squares_of(held_tiles, select(weights.reshape(rows_dev, tile_rows), row_in)),
        precision=lax.Precision.HIGHEST,
    ).reshape(src_dev)
    grad_sum, diag_sum = (
        lax.psum_scatter(grad_part, ("rcv", "tw"), scatter_dimension=0, tiled=True),
        lax.psum_scatter(diag_part, ("rcv", "tw"), scatter_dimension=0, tiled=True),
    )
    share_rows = grad_sum.shape[0]
    share_index = owner_index * columns + column_index
    model_share = lax.dynamic_slice_in_dim(source_model, share_index * share_rows, share_rows, 0)
    residual = grad_sum - damping * model_share
    precond = diag_sum + damping
    scaled = residual / precond[:, None]
    inner = member_total(jnp.sum(residual * scaled, axis=0))
    direction = scaled
    model_update = jnp.zeros_like(residual)
    for sweep in range(CG_ITERS):
        direction_full = lax.all_gather(
            direction.astype(jnp.bfloat16), ("rcv", "tw"), axis=0, tiled=True
        )
        image_rows, unused_offset = settle(
            forward(direction_full.reshape(blocks_src, block_src, members)).reshape(
                gauges_dev, samples_dev, members
            )
        )
        weighted = (robust * image_rows).astype(jnp.bfloat16).reshape(rows_dev, tile_rows, members)
        curvature = (
            lax.psum_scatter(
                adjoint(weighted).reshape(src_dev, members),
                ("rcv", "tw"),
                scatter_dimension=0,
                tiled=True,
            )
            + damping * direction
        )
        step_size = inner / member_total(jnp.sum(direction * curvature, axis=0))
        model_update = model_update + step_size * direction
        if sweep + 1 < CG_ITERS:
            residual = residual - step_size * curvature
            scaled = residual / precond[:, None]
            inner_next = member_total(jnp.sum(residual * scaled, axis=0))
            direction = scaled + inner_next / inner * direction
            inner = inner_next
    return model_update.reshape(1, share_rows, members)


def solution(mesh):
    placed = (
        P(("scen", "rcv"), "src", "tw", None, None),
        P("scen", "src", "tw", None),
        P("scen", "src", "tw", None),
        P(("scen", "rcv"), "tw", None),
        P(("scen", "rcv"), "tw"),
        P(("scen", "src"), None),
    )
    return jax.shard_map(
        shards,
        mesh=mesh,
        in_specs=placed,
        out_specs=P(("scen", "src"), ("rcv", "tw"), None),
        check_vma=False,
    )
```

profile of v0, /device:TPU:0, one launch (start us, length us, event | category | flops | bytes accessed | tf_op | source)
XLA Modules:
  0.0 560.1 jit_solution(3874980222967234504)
XLA Ops:
  15.0 6.3 %all-to-all-start = ((bf16[64,128,128]{2,1,0:T(8,128)(2,1)}), bf16[64,128,128]{2,1,0:T(8,128)(2,1)S(1)}, u32[]{:S(2)}, u32[]{:S(2)}) async-start(bf16[64,128,128]{2,1,0:T(8,128)(2,1)} %select_select_fusion), calls=%async_computation | async-start | bytes 4194304 | tf_op jit(solution)/shard_map/all_to_all | solution.py:82
  24.0 2.1 gather_fusion.4
  26.5 43.0 %all-to-all-done = bf16[64,128,128]{2,1,0:T(8,128)(2,1)S(1)} async-done(((bf16[64,128,128]{2,1,0:T(8,128)(2,1)}), bf16[64,128,128]{2,1,0:T(8,128)(2,1)S(1)}, u32[]{:S(2)}, u32[]{:S(2)}) %all-to-all-start) | async-done | bytes 2097184 | tf_op jit(solution)/shard_map/all_to_all | solution.py:82
  69.5 4.3 fusion.13
  73.9 8.8 %scatter_fusion = f32[16,128,128]{2,1,0:T(8,128)S(1)} fusion(f32[16,128,128]{2,1,0:T(8,128)S(1)} %broadcast.224.clone, s32[64]{0:T(128)S(1)} %get-tuple-element.14, f32[64,128,128]{2,1,0:T(8,128)} %fusion.13), kind=kCustom, calls=%fused_computation.10 | custom fusion | flops 1048576 | bytes 12583168 | tf_op jit(solution)/shard_map/scatter-add | solution.py:22
  83.8 39.3 %all-reduce.6.cloned.1.call-done = f32[4,512,128]{2,1,0:T(8,128)} async-done(((f32[4,512,128]{2,1,0:T(8,128)}), f32[4,512,128]{2,1,0:T(8,128)}) %all-reduce.6.cloned.1.call-update) | async-done | bytes 1048592 | tf_op jit(solution)/shard_map/psum | solution.py:101
  124.7 2.1 gather_fusion.5
  126.9 4.5 fusion.11
  132.9 13.5 %scatter_fusion.1 = f32[32,128,128]{2,1,0:T(8,128)} fusion(f32[32,128,128]{2,1,0:T(8,128)} %broadcast.218.clone, s32[64]{0:T(128)S(1)} %get-tuple-element.13, f32[64,128,128]{2,1,0:T(8,128)} %fusion.11), kind=kCustom, calls=%fused_computation.11 | custom fusion | flops 1048576 | bytes 12583168 | tf_op jit(solution)/shard_map/scatter-add | solution.py:22
  148.4 3.5 fusion
  152.1 29.1 %all-reduce = f32[4096]{0:T(1024)S(1)} all-reduce(f32[4096]{0:T(1024)S(1)} %convolution_bitcast_fusion), channel_id=3, replica_groups=mesh['scen'=2,'rcv'=4,'src'=2,'tw'=2] {'rcv','tw'}, use_global_device_ids=true, to_apply=%region_5.9.clone | all-reduce | flops 4096 | bytes 32768
  184.2 20.9 %all-gather.3.cloned.1.call-done = bf16[4096,128]{1,0:T(8,128)(2,1)} async-done(((bf16[512,128]{1,0:T(8,128)(2,1)}), bf16[4096,128]{1,0:T(8,128)(2,1)}) %all-gather.3.cloned.1.call-update) | async-done | bytes 1048592 | tf_op jit(solution)/shard_map/all_gather | solution.py:132
  205.0 3.4 gather_fusion.6
  208.4 4.3 fusion.9
  212.8 8.8 %scatter_fusion.2 = f32[16,128,128]{2,1,0:T(8,128)S(1)} fusion(f32[16,128,128]{2,1,0:T(8,128)S(1)} %broadcast.224.clone.1, s32[64]{0:T(128)S(1)} %get-tuple-element.14, f32[64,128,128]{2,1,0:T(8,128)} %fusion.9), kind=kCustom, calls=%fused_computation.12 | custom fusion | flops 1048576 | bytes 12583168 | tf_op jit(solution)/shard_map/scatter-add | solution.py:22
  222.7 39.7 %all-reduce.8.cloned.1.call-done = f32[4,512,128]{2,1,0:T(8,128)} async-done(((f32[4,512,128]{2,1,0:T(8,128)}), f32[4,512,128]{2,1,0:T(8,128)}) %all-reduce.8.cloned.1.call-update) | async-done | bytes 1048592 | tf_op jit(solution)/shard_map/psum | solution.py:101
  264.5 2.1 gather_fusion.7
  266.6 4.5 fusion.7
  272.6 13.5 %scatter_fusion.3 = f32[32,128,128]{2,1,0:T(8,128)} fusion(f32[32,128,128]{2,1,0:T(8,128)} %broadcast.218.clone.1, s32[64]{0:T(128)S(1)} %get-tuple-element.13, f32[64,128,128]{2,1,0:T(8,128)} %fusion.7), kind=kCustom, calls=%fused_computation.13 | custom fusion | flops 1048576 | bytes 12583168 | tf_op jit(solution)/shard_map/scatter-add | solution.py:22
  286.2 35.8 %reduce-scatter.6.cloned.1.call-done = f32[512,128]{1,0:T(8,128)} async-done(((f32[4096,128]{1,0:T(8,128)}), f32[512,128]{1,0:T(8,128)}) %reduce-scatter.6.cloned.1.call-update) | async-done | bytes 262160 | tf_op jit(solution)/shard_map/reduce_scatter | solution.py:142
  323.1 31.4 %all-reduce.1 = (f32[128]{0:T(128)S(1)}, f32[128]{0:T(128)S(1)}) all-reduce(f32[128]{0:T(128)S(1)} %get-tuple-element.8, f32[128]{0:T(128)S(1)} %get-tuple-element.6), channel_id=1, replica_groups=mesh['scen'=2,'rcv'=4,'src'=2,'tw'=2] {'rcv','src','tw'}, use_global_device_ids=true, to_apply=%region_7.11 | all-reduce | flops 256 | bytes 2048 | tf_op jit(solution)/shard_map/psum | solution.py:104
  355.6 29.5 %psum.53 = f32[128]{0:T(128)S(1)} all-reduce(f32[128]{0:T(128)S(1)} %multiply_reduce_fusion.1), channel_id=1, replica_groups=mesh['scen'=2,'rcv'=4,'src'=2,'tw'=2] {'rcv','src','tw'}, use_global_device_ids=true, to_apply=%region_15.19 | all-reduce | flops 128 | bytes 1024 | tf_op jit(solution)/shard_map/psum | solution.py:104
  387.1 19.4 %all-gather.5.cloned.1.call-done = bf16[4096,128]{1,0:T(8,128)(2,1)} async-done(((bf16[512,128]{1,0:T(8,128)(2,1)}), bf16[4096,128]{1,0:T(8,128)(2,1)}) %all-gather.5.cloned.1.call-update) | async-done | bytes 1048592 | tf_op jit(solution)/shard_map/all_gather | solution.py:132
  406.5 3.4 gather_fusion.8
  409.9 4.3 fusion.5
  414.3 8.8 %scatter_fusion.4 = f32[16,128,128]{2,1,0:T(8,128)S(1)} fusion(f32[16,128,128]{2,1,0:T(8,128)S(1)} %broadcast.224, s32[64]{0:T(128)S(1)} %get-tuple-element.14, f32[64,128,128]{2,1,0:T(8,128)} %fusion.5), kind=kCustom, calls=%fused_computation.14 | custom fusion | flops 1048576 | bytes 12583168 | tf_op jit(solution)/shard_map/scatter-add | solution.py:22
  424.2 39.8 %all-reduce.10.cloned.1.call-done = f32[4,512,128]{2,1,0:T(8,128)} async-done(((f32[4,512,128]{2,1,0:T(8,128)}), f32[4,512,128]{2,1,0:T(8,128)}) %all-reduce.10.cloned.1.call-update) | async-done | bytes 1048592 | tf_op jit(solution)/shard_map/psum | solution.py:101
  466.0 2.1 gather_fusion.9
  468.1 4.5 fusion.3
  472.8 8.8 %scatter_fusion.5 = f32[32,128,128]{2,1,0:T(8,128)S(1)} fusion(f32[32,128,128]{2,1,0:T(8,128)S(1)} %broadcast.218, s32[64]{0:T(128)S(1)} %get-tuple-element.13, f32[64,128,128]{2,1,0:T(8,128)} %fusion.3), kind=kCustom, calls=%fused_computation.15 | custom fusion | flops 1048576 | bytes 12583168 | tf_op jit(solution)/shard_map/scatter-add | solution.py:22
  483.0 35.9 %reduce-scatter.8.cloned.1.call-done = f32[512,128]{1,0:T(8,128)} async-done(((f32[4096,128]{1,0:T(8,128)}), f32[512,128]{1,0:T(8,128)}) %reduce-scatter.8.cloned.1.call-update) | async-done | bytes 262160 | tf_op jit(solution)/shard_map/reduce_scatter | solution.py:142
  520.0 31.4 %psum.55 = f32[128]{0:T(128)S(1)} all-reduce(f32[128]{0:T(128)S(1)} %multiply_reduce_fusion), channel_id=1, replica_groups=mesh['scen'=2,'rcv'=4,'src'=2,'tw'=2] {'rcv','src','tw'}, use_global_device_ids=true, to_apply=%region_21.25 | all-reduce | flops 128 | bytes 1024 | tf_op jit(solution)/shard_map/psum | solution.py:104
  (97 shorter events, 36.9 us)
Async XLA Ops:
  6.5 5.8 %copy-start = (bf16[32,1,1,128,128]{4,3,2,1,0:T(8,128)(2,1)S(1)}, bf16[32,1,1,128,128]{4,3,2,1,0:T(8,128)(2,1)}, u32[]{:S(2)}) copy-start(bf16[32,1,1,128,128]{4,3,2,1,0:T(8,128)(2,1)} %param.12) | copy-start | bytes 3145732
  15.0 54.5 %all-to-all-start = ((bf16[64,128,128]{2,1,0:T(8,128)(2,1)}), bf16[64,128,128]{2,1,0:T(8,128)(2,1)S(1)}, u32[]{:S(2)}, u32[]{:S(2)}) async-start(bf16[64,128,128]{2,1,0:T(8,128)(2,1)} %select_select_fusion), calls=%async_computation | async-start | bytes 4194304 | tf_op jit(solution)/shard_map/all_to_all | solution.py:82
  21.3 101.7 %all-reduce.6.cloned.1.call-start = ((), (), s32[]{:S(2)}) async-start(), calls=%async_computation.4 | async-start | bytes 2097152 | tf_op jit(solution)/shard_map/psum | solution.py:101
  73.9 49.1 %copy-start.6 = (f32[4,512]{1,0:T(4,128)S(1)}, f32[4,512]{1,0:T(4,128)}, u32[]{:S(2)}) copy-start(f32[4,512]{1,0:T(4,128)} %param.16) | copy-start | bytes 24580
  82.7 1.0 copy-start.3
  83.7 98.4 %reduce-scatter.4.cloned.1.call-start = ((), (), s32[]{:S(2)}) async-start(), calls=%async_computation.5 | async-start | bytes 2359296 | tf_op jit(solution)/shard_map/reduce_scatter | solution.py:119
  146.4 0.7 copy-start.7
  146.4 58.6 %all-gather.3.cloned.1.call-start = ((), (), s32[]{:S(2)}) async-start(), calls=%async_computation.6 | async-start | bytes 1179648 | tf_op jit(solution)/shard_map/all_gather | solution.py:132
  183.9 78.5 %all-reduce.8.cloned.1.call-start = ((), (), s32[]{:S(2)}) async-start(), calls=%async_computation.7 | async-start | bytes 2097152 | tf_op jit(solution)/shard_map/psum | solution.py:101
  221.6 1.0 copy-start.4
  222.6 99.3 %reduce-scatter.6.cloned.1.call-start = ((), (), s32[]{:S(2)}) async-start(), calls=%async_computation.8 | async-start | bytes 2359296 | tf_op jit(solution)/shard_map/reduce_scatter | solution.py:142
  286.2 120.3 %all-gather.5.cloned.1.call-start = ((), (), s32[]{:S(2)}) async-start(), calls=%async_computation.9 | async-start | bytes 1179648 | tf_op jit(solution)/shard_map/all_gather | solution.py:132
  387.0 76.9 %all-reduce.10.cloned.1.call-start = ((), (), s32[]{:S(2)}) async-start(), calls=%async_computation.10 | async-start | bytes 2097152 | tf_op jit(solution)/shard_map/psum | solution.py:101
  423.1 1.0 copy-start.2
  424.1 94.8 %reduce-scatter.8.cloned.1.call-start = ((), (), s32[]{:S(2)}) async-start(), calls=%async_computation.11 | async-start | bytes 2359296 | tf_op jit(solution)/shard_map/reduce_scatter | solution.py:142
  472.8 80.5 %copy-start.1 = (bf16[32,1,1,128,128]{4,3,2,1,0:T(8,128)(2,1)S(1)}, bf16[32,1,1,128,128]{4,3,2,1,0:T(8,128)(2,1)}, u32[]{:S(2)}) copy-start(bf16[32,1,1,128,128]{4,3,2,1,0:T(8,128)(2,1)} %param.12) | copy-start | bytes 3145732
  481.6 1.4 copy-start.5
Sparse Core Ops, SparseCore 0:
  83.8 39.1 all-reduce.5
  146.6 35.4 reduce-scatter.3
  184.0 20.9 all-gather.2
  222.8 39.6 all-reduce.7
  286.3 35.6 reduce-scatter.5
  387.1 19.3 all-gather.4
  424.3 39.6 all-reduce.9
  483.1 35.7 reduce-scatter.7
where the time goes:
time: 562 us; the launch traced here: 560 us
  waiting for transfers between devices  275 us (49%)
  blocking collectives  121 us (22%)
  other arithmetic  83.1 us (15%)
  matrix products  29.9 us (5%)
  local copies, waits for them, and re-layouts  29.8 us (5%)
  between operations  14.5 us (3%)
  starting transfers between devices  6.79 us (1%)
    psum x3, waiting for transfers between devices, settle(): return (lax.psum(partial_rows, 'src'), 0)  119 us
    psum x3, blocking collectives, member_total(): return lax.psum(vector, ('rcv', 'src', 'tw'))  92.3 us
    reduce_scatter x2, waiting for transfers between devices, shards(): lax.psum_scatter(adjoint(weighted).reshape(src_dev, members), ('rcv', 'tw...  71.7 us
    scatter-add x6, other arithmetic, spread(): return jax.ops.segment_sum(values, target, num_segments=length)  62.2 us
    all_to_all x1, waiting for transfers between devices, shards(): lax.all_to_all(slot_tiles, 'rcv', split_axis=0, concat_axis=0, tiled=True)  43 us
    all_gather x2, waiting for transfers between devices, shards(): lax.all_gather(direction.astype(jnp.bfloat16), ('rcv', 'tw'), axis=0, til...  40.3 us
    unnamed x1, blocking collectives  29.1 us
    gather x7, local copies, waits for them, and re-layouts, select(): return jnp.take(values, jnp.maximum(indices, 0), axis=0)  15.9 us
  transfers between devices with their start and end apart: 9, of which 9 were waited for; matrix products, arithmetic and copies ran while one was open for 2% of the time, Pallas kernels for 0%

commit v1 on v0

v1 whole, which is shorter than its diff:
```python
import functools

import jax
import jax.numpy as jnp
from jax import lax
from jax.experimental import pallas as pl
from jax.experimental.pallas import tpu as pltpu
from jax.sharding import PartitionSpec as P

damping = 0.5
CHUNKS = 4
UNROLL = 8
MESH = pl.DeviceIdType.MESH
F32 = jnp.float32
BF16 = jnp.bfloat16


def remote(src, dst, send, recv, axis, index):
    return pltpu.make_async_remote_copy(
        src_ref=src,
        dst_ref=dst,
        send_sem=send,
        recv_sem=recv,
        device_id={axis: index},
        device_id_type=MESH,
    )


def kernel(
    sizes,
    f_tile, f_src, f_keep, f_last, f_has, a_tile, a_row, a_keep, a_last, a_has,
    tiles, model_half, model_share, observed, weights,
    out,
    prod, psq, own, robust, data, xsend, xrecv, ksend, krecv, zsend, zrecv,
    dksend, dkrecv, dzsend, dzrecv, gsend, gfull, d0, e0, precond, vec, vrecv,
    xs_sem, xr_sem, ks_sem, kr_sem, zs_sem, zr_sem, dks_sem, dkr_sem, dzs_sem, dzr_sem,
    gs_sem, gr_sem, hs_sem, hr_sem, vs_sem, vr_sem,
):
    R, S, T, slots, rows, blocks, bs = sizes
    r, j, k = lax.axis_index("rcv"), lax.axis_index("src"), lax.axis_index("tw")
    sib = 1 - k
    per = rows // CHUNKS
    drain = []

    barrier = pltpu.get_barrier_semaphore()
    pl.semaphore_signal(barrier, inc=1, device_id={"tw": sib}, device_id_type=MESH)
    for i in range(1, R):
        pl.semaphore_signal(
            barrier, inc=1, device_id={"rcv": lax.rem(r + i, R)}, device_id_type=MESH
        )
    for i in range(1, S):
        pl.semaphore_signal(
            barrier, inc=1, device_id={"src": lax.rem(j + i, S)}, device_id_type=MESH
        )
    pl.semaphore_wait(barrier, R + S - 1)

    def forward(load):
        def body(step, acc):
            for u in range(UNROLL):
                t = step * UNROLL + u
                acc = acc * f_keep[t] + jnp.dot(
                    tiles[f_tile[t]], load(f_src[t]), preferred_element_type=F32
                )
                prod[t] = acc
            return acc

        lax.fori_loop(0, slots // UNROLL, body, jnp.zeros(prod.shape[1:], F32))

    def adjoint(with_squares):
        def body(step, carry):
            acc, sq = carry
            for u in range(UNROLL):
                t = step * UNROLL + u
                tile = tiles[a_tile[t]]
                acc = acc * a_keep[t] + lax.dot_general(
                    tile, data[a_row[t]], (((0,), (0,)), ((), ())), preferred_element_type=F32
                )
                prod[t] = acc
                if with_squares:
                    wide = tile.astype(F32)
                    term = wide * wide * weights[a_row[t]]
                    term = jnp.sum(term.reshape(term.shape[0] // 8, 8, term.shape[1]), axis=0)
                    sq = sq * a_keep[t] + term
                    psq[t] = sq
            return acc, sq

        lax.fori_loop(
            0,
            slots // UNROLL,
            body,
            (jnp.zeros(prod.shape[1:], F32), jnp.zeros(psq.shape[1:], F32)),
        )

    def xchunk(rnd, i, c):
        return remote(
            xsend.at[rnd, pl.ds(c * per, per)],
            xrecv.at[rnd, i - 1, pl.ds(c * per, per)],
            xs_sem.at[rnd, i - 1, c],
            xr_sem.at[rnd, i - 1, c],
            "src",
            lax.rem(j + i, S),
        )

    def exchange(rnd, use):
        for c in range(CHUNKS):
            for row in range(c * per, (c + 1) * per):
                value = prod[f_last[row]] * f_has[row]
                own[row] = value
                xsend[rnd, row] = value.astype(BF16)
            for i in range(1, S):
                copy = xchunk(rnd, i, c)
                copy.start()
                drain.append(copy)
        for c in range(CHUNKS):
            for i in range(1, S):
                xchunk(rnd, i, c).wait_recv()
            for row in range(c * per, (c + 1) * per):
                total = own[row]
                for i in range(1, S):
                    total = total + xrecv[rnd, i - 1, row].astype(F32)
                use(row, total)

    def kcopy(rnd, i):
        return remote(
            ksend.at[rnd, i], krecv.at[rnd, i], ks_sem.at[rnd, i], kr_sem.at[rnd, i], "tw", sib
        )

    def zcopy(rnd, i):
        return remote(
            zsend.at[rnd, i], zrecv.at[rnd, i], zs_sem.at[rnd, i], zr_sem.at[rnd, i],
            "rcv", lax.rem(r + i, R),
        )

    def dkcopy():
        return remote(dksend, dkrecv, dks_sem.at[0], dkr_sem.at[0], "tw", sib)

    def dzcopy(i):
        return remote(
            dzsend.at[i], dzrecv.at[i], dzs_sem.at[i], dzr_sem.at[i], "rcv", lax.rem(r + i, R)
        )

    order = list(range(1, R)) + [0]

    def scatter(rnd):
        for i in order:
            chip = lax.rem(r + i, R)
            for b in range(bs):
                block = (chip * T + sib) * bs + b
                ksend[rnd, i, b] = prod[a_last[block]] * a_has[block]
            copy = kcopy(rnd, i)
            copy.start()
            drain.append(copy)
        if rnd == 0:
            for i in range(R):
                chip = lax.rem(r + i, R)
                for b in range(bs):
                    block = (chip * T + sib) * bs + b
                    dksend[i, b] = psq[a_last[block]] * a_has[block]
            copy = dkcopy()
            copy.start()
            drain.append(copy)
        for i in order:
            chip = lax.rem(r + i, R)
            kcopy(rnd, i).wait_recv()
            for b in range(bs):
                block = (chip * T + k) * bs + b
                value = prod[a_last[block]] * a_has[block] + krecv[rnd, i, b]
                if i == 0:
                    own[b] = value
                else:
                    zsend[rnd, i, b] = value.astype(BF16)
            if i > 0:
                copy = zcopy(rnd, i)
                copy.start()
                drain.append(copy)
        if rnd == 0:
            dkcopy().wait_recv()
            for i in range(R):
                chip = lax.rem(r + i, R)
                for b in range(bs):
                    block = (chip * T + k) * bs + b
                    dzsend[i, b] = psq[a_last[block]] * a_has[block] + dkrecv[i, b]
                if i > 0:
                    copy = dzcopy(i)
                    copy.start()
                    drain.append(copy)
            for i in range(1, R):
                dzcopy(i).wait_recv()
            for b in range(bs):
                total = dzsend[0, b]
                for i in range(1, R):
                    total = total + dzrecv[i, b]
                line = jnp.sum(total, axis=0, keepdims=True)
                wide = jnp.broadcast_to(line, precond.shape[1:])
                precond[b] = wide.T + damping
        for i in range(1, R):
            zcopy(rnd, i).wait_recv()
        result = []
        for b in range(bs):
            total = own[b]
            for i in range(1, R):
                total = total + zrecv[rnd, i, b].astype(F32)
            result.append(total)
        return result

    def place(chip, core):
        return pl.ds((chip * T + core) * bs, bs)

    def gather(rnd):
        mine = place(r, k)
        gfull[rnd, mine] = gsend[rnd]

        def zc(i):
            return remote(
                gsend.at[rnd], gfull.at[rnd, mine],
                gs_sem.at[rnd, i], gr_sem.at[rnd, i], "rcv", lax.rem(r + i, R),
            )

        def zwait(i):
            spot = place(lax.rem(r + R - i, R), k)
            remote(
                gsend.at[rnd], gfull.at[rnd, spot],
                gs_sem.at[rnd, i], gr_sem.at[rnd, i], "rcv", lax.rem(r + i, R),
            ).wait_recv()

        def hc(i, core):
            spot = place(lax.rem(r + R - i, R), core)
            return remote(
                gfull.at[rnd, spot], gfull.at[rnd, spot],
                hs_sem.at[rnd, i], hr_sem.at[rnd, i], "tw", sib,
            )

        for i in range(1, R):
            copy = zc(i)
            copy.start()
            drain.append(copy)
        for i in range(R):
            if i > 0:
                zwait(i)
            copy = hc(i, k)
            copy.start()
            drain.append(copy)
        for i in range(R):
            hc(i, sib).wait_recv()

    forward(lambda s: model_half[s])

    def first(row, predicted):
        misfit = observed[row].astype(F32) - predicted
        weight = weights[row] / (1.0 + misfit * misfit)
        robust[row] = weight
        data[row] = (weight * misfit).astype(BF16)

    exchange(0, first)
    adjoint(True)
    grad = scatter(0)
    inner0 = jnp.zeros((1, out.shape[2]), F32)
    for b in range(bs):
        residual = grad[b] - damping * model_share[b]
        scaled = residual / precond[b]
        inner0 = inner0 + jnp.sum(residual * scaled, axis=0, keepdims=True)
        d0[b] = scaled
        gsend[0, b] = scaled.astype(BF16)
    gather(0)

    forward(lambda s: gfull[0, s])

    def second(row, image):
        data[row] = (robust[row] * image).astype(BF16)

    exchange(1, second)
    adjoint(False)
    curve = scatter(1)
    dc = jnp.zeros_like(inner0)
    ce = jnp.zeros_like(inner0)
    ee = jnp.zeros_like(inner0)
    for b in range(bs):
        direction = d0[b]
        curvature = curve[b] + damping * direction
        scaled = curvature / precond[b]
        dc = dc + jnp.sum(direction * curvature, axis=0, keepdims=True)
        ce = ce + jnp.sum(curvature * scaled, axis=0, keepdims=True)
        ee = ee + jnp.sum(scaled * scaled, axis=0, keepdims=True)
        e0[b] = scaled
        gsend[1, b] = scaled.astype(BF16)
    gather(1)

    forward(lambda s: gfull[1, s])
    part = rows // S

    def lastcopy(i):
        other = lax.rem(j + i, S)
        return remote(
            xsend.at[2, pl.ds(other * part, part)],
            xrecv.at[2, i - 1, pl.ds(0, part)],
            xs_sem.at[2, i - 1, 0],
            xr_sem.at[2, i - 1, 0],
            "src",
            other,
        )

    for i in range(1, S):
        other = lax.rem(j + i, S)
        for n in range(part):
            row = other * part + n
            xsend[2, row] = (prod[f_last[row]] * f_has[row]).astype(BF16)
        copy = lastcopy(i)
        copy.start()
        drain.append(copy)
    for i in range(1, S):
        lastcopy(i).wait_recv()
    quad = jnp.zeros_like(inner0)
    for n in range(part):
        row = j * part + n
        image = prod[f_last[row]] * f_has[row]
        for i in range(1, S):
            image = image + xrecv[2, i - 1, n].astype(F32)
        quad = quad + jnp.sum(robust[row] * image * image, axis=0, keepdims=True)

    values = jnp.concatenate(
        [inner0, dc, ce, quad + damping * ee, jnp.zeros((4, inner0.shape[1]), F32)], axis=0
    )
    base = 0
    for stage, (axis, me, n) in enumerate((("tw", k, T), ("rcv", r, R), ("src", j, S))):
        vec[stage] = values
        copies = []
        for i in range(1, n):
            copy = remote(
                vec.at[stage], vrecv.at[base + i - 1],
                vs_sem.at[base + i - 1], vr_sem.at[base + i - 1], axis, lax.rem(me + i, n),
            )
            copy.start()
            drain.append(copy)
            copies.append(copy)
        for i, copy in enumerate(copies):
            copy.wait_recv()
            values = values + vrecv[base + i]
        base += n - 1
    inner0, dc, ce, eae = (values[n : n + 1] for n in range(4))
    step0 = inner0 / dc
    inner1 = inner0 - 2.0 * step0 * dc + step0 * step0 * ce
    grow = 1.0 + inner1 / inner0
    bend = grow * grow * dc - 2.0 * grow * step0 * ce + step0 * step0 * eae
    step1 = inner1 / bend
    for b in range(bs):
        direction = d0[b]
        out[b] = step0 * direction + step1 * (grow * direction - step0 * e0[b])
    for copy in drain:
        copy.wait_send()


def listing_of(key, other, groups):
    slots = key.shape[0]
    ids = jnp.arange(slots, dtype=jnp.int32)
    before = (key[None, :] < key[:, None]) | (
        (key[None, :] == key[:, None]) & (ids[None, :] < ids[:, None])
    )
    rank = jnp.sum(before.astype(jnp.int32), axis=1)
    hit = rank[None, :] == ids[:, None]
    order = jnp.sum(jnp.where(hit, ids[None, :], 0), axis=1)
    partner = jnp.sum(jnp.where(hit, other[None, :], 0), axis=1)
    sorted_key = jnp.sum(jnp.where(hit, key[None, :], 0), axis=1)
    keep = jnp.concatenate(
        [jnp.zeros((1,), F32), (sorted_key[1:] == sorted_key[:-1]).astype(F32)]
    )
    group_ids = jnp.arange(groups, dtype=jnp.int32)
    upto = jnp.sum((key[None, :] <= group_ids[:, None]).astype(jnp.int32), axis=1)
    count = jnp.sum((key[None, :] == group_ids[:, None]).astype(jnp.int32), axis=1)
    return order, partner, keep, jnp.maximum(upto - 1, 0), (count > 0).astype(F32)


def shards(green_tiles, arrivals, counts, observed, weights, source_model):
    own_tiles = green_tiles.reshape(
        green_tiles.shape[0], green_tiles.shape[3], green_tiles.shape[4]
    )
    tiles_dev, tile_rows, block_src = own_tiles.shape
    listing = arrivals.reshape(arrivals.shape[0], 3)
    owners = lax.axis_size("rcv")
    columns = lax.axis_size("tw")
    sources = lax.axis_size("src")
    counts_all = counts.reshape(owners, owners)
    starts = jnp.cumsum(counts_all, axis=1) - counts_all
    gauges_dev, samples_dev, members = observed.shape
    blocks_col = samples_dev // tile_rows
    rows_dev = gauges_dev * blocks_col
    src_dev = source_model.shape[0]
    blocks_src = src_dev // block_src
    capacity = 2 * tiles_dev // owners
    slots = capacity * owners
    owner_index = lax.axis_index("rcv")
    source_index = lax.axis_index("src")
    column_index = lax.axis_index("tw")
    slot_ids = jnp.arange(capacity, dtype=jnp.int32)
    holder_ids = jnp.arange(owners, dtype=jnp.int32)
    count_in = lax.dynamic_slice_in_dim(counts_all, owner_index, 1, 1)[:, 0]
    start_in = lax.dynamic_slice_in_dim(starts, owner_index, 1, 1)[:, 0]
    local_in = start_in[:, None] + slot_ids[None, :]
    valid_in = (slot_ids[None, :] < count_in[:, None]) & (local_in < tiles_dev)
    index_in = jnp.where(valid_in, holder_ids[:, None] * tiles_dev + local_in, 0).reshape(-1)
    listed_in = jnp.take(listing, index_in, axis=0)
    valid_in = valid_in.reshape(-1) & (listed_in[:, 0] // gauges_dev == owner_index)
    row_in = jnp.where(
        valid_in,
        (listed_in[:, 0] - owner_index * gauges_dev) * blocks_col
        + listed_in[:, 2]
        - column_index * blocks_col,
        rows_dev,
    )
    block_in = jnp.where(valid_in, listed_in[:, 1] - source_index * blocks_src, blocks_src)
    count_out = lax.dynamic_slice_in_dim(counts_all, owner_index, 1, 0)[0]
    start_out = lax.dynamic_slice_in_dim(starts, owner_index, 1, 0)[0]
    local_out = start_out[:, None] + slot_ids[None, :]
    valid_out = (slot_ids[None, :] < count_out[:, None]) & (local_out < tiles_dev)
    index_out = jnp.where(valid_out, local_out, 0).reshape(-1)
    slot_tiles = jnp.take(own_tiles, index_out, axis=0)
    held_tiles = lax.all_to_all(slot_tiles, "rcv", split_axis=0, concat_axis=0, tiled=True)
    by_row = listing_of(row_in, jnp.minimum(block_in, blocks_src - 1), rows_dev)
    by_block = listing_of(block_in, jnp.minimum(row_in, rows_dev - 1), blocks_src)

    share = blocks_src // (owners * columns)
    share_index = owner_index * columns + column_index
    model_blocks = source_model.reshape(blocks_src, block_src, members)
    model_share = lax.dynamic_slice_in_dim(model_blocks, share_index * share, share, 0)
    weight_wide = jnp.broadcast_to(
        weights.reshape(rows_dev, tile_rows, 1), (rows_dev, tile_rows, members)
    )
    sizes = (owners, sources, columns, slots, rows_dev, blocks_src, share)
    full = (block_src, members)
    eight = (8, block_src)
    peers = max(sources - 1, 1)
    stages = columns + owners + sources - 3
    dma = pltpu.SemaphoreType.DMA
    scratch = [
        pltpu.VMEM((slots,) + full, F32),
        pltpu.VMEM((slots,) + eight, F32),
        pltpu.VMEM((rows_dev,) + full, F32),
        pltpu.VMEM((rows_dev,) + full, F32),
        pltpu.VMEM((rows_dev,) + full, BF16),
        pltpu.VMEM((3, rows_dev) + full, BF16),
        pltpu.VMEM((3, peers, rows_dev) + full, BF16),
        pltpu.VMEM((2, owners, share) + full, F32),
        pltpu.VMEM((2, owners, share) + full, F32),
        pltpu.VMEM((2, owners, share) + full, BF16),
        pltpu.VMEM((2, owners, share) + full, BF16),
        pltpu.VMEM((owners, share) + eight, F32),
        pltpu.VMEM((owners, share) + eight, F32),
        pltpu.VMEM((owners, share) + eight, F32),
        pltpu.VMEM((owners, share) + eight, F32),
        pltpu.VMEM((2, share) + full, BF16),
        pltpu.VMEM((2, blocks_src) + full, BF16),
        pltpu.VMEM((share,) + full, F32),
        pltpu.VMEM((share,) + full, F32),
        pltpu.VMEM((share,) + full, F32),
        pltpu.VMEM((3, 8, members), F32),
        pltpu.VMEM((stages, 8, members), F32),
        dma((3, peers, CHUNKS)), dma((3, peers, CHUNKS)),
        dma((2, owners)), dma((2, owners)),
        dma((2, owners)), dma((2, owners)),
        dma((1,)), dma((1,)),
        dma((owners,)), dma((owners,)),
        dma((2, owners)), dma((2, owners)),
        dma((2, owners)), dma((2, owners)),
        dma((stages,)), dma((stages,)),
    ]
    vmem = pl.BlockSpec(memory_space=pltpu.VMEM)
    smem = pl.BlockSpec(memory_space=pltpu.SMEM)
    update = pl.pallas_call(
        functools.partial(kernel, sizes),
        out_shape=jax.ShapeDtypeStruct((share,) + full, F32),
        in_specs=[smem] * 10 + [vmem] * 5,
        out_specs=vmem,
        scratch_shapes=scratch,
        compiler_params=pltpu.CompilerParams(
            collective_id=0, has_side_effects=True, vmem_limit_bytes=48 * 1024 * 1024
        ),
    )(
        *by_row,
        *by_block,
        held_tiles,
        model_blocks.astype(BF16),
        model_share,
        observed.reshape(rows_dev, tile_rows, members),
        weight_wide,
    )
    return update.reshape(1, share * block_src, members)


def solution(mesh):
    placed = (
        P(("scen", "rcv"), "src", "tw", None, None),
        P("scen", "src", "tw", None),
        P("scen", "src", "tw", None),
        P(("scen", "rcv"), "tw", None),
        P(("scen", "rcv"), "tw"),
        P(("scen", "src"), None),
    )
    return jax.shard_map(
        shards,
        mesh=mesh,
        in_specs=placed,
        out_specs=P(("scen", "src"), ("rcv", "tw"), None),
        check_vma=False,
    )
```

time: 562 us -> 175 us (0.31)
  waiting for transfers between devices: 275 us -> 41.8 us
  blocking collectives: 121 us -> 0 us
  Pallas kernels: 0 us -> 109 us
  other arithmetic: 83.1 us -> 8.09 us
  matrix products: 29.9 us -> 0 us
  local copies, waits for them, and re-layouts: 29.8 us -> 8.42 us
  between operations: 14.5 us -> 0.19 us
    psum x3 -> x0, waiting for transfers between devices: 119 us -> none  [settle(): return (lax.psum(partial_rows, 'src'), 0)]
    pallas_call x0 -> x1, Pallas kernels: none -> 109 us  [shards(): pl.pallas_call(functools.partial(kernel, sizes), out_shape=jax.ShapeDtype...]
    psum x3 -> x0, blocking collectives: 92.3 us -> none  [member_total(): return lax.psum(vector, ('rcv', 'src', 'tw'))]
    reduce_scatter x3 -> x0, waiting for transfers between devices: 72.5 us -> none  [the longest x2 71.7 us: shards(): lax.psum_scatter(adjoint(weighted).reshape(src_dev, members), ('rcv', 'tw...]
    scatter-add x6 -> x0, other arithmetic: 62.2 us -> none  [spread(): return jax.ops.segment_sum(values, target, num_segments=length)]
    all_gather x2 -> x0, waiting for transfers between devices: 40.3 us -> none  [shards(): lax.all_gather(direction.astype(jnp.bfloat16), ('rcv', 'tw'), axis=0, til...]
    dot_general x8 -> x0, matrix products: 29.9 us -> none  [the longest x3 13.4 us: adjoint(): jnp.einsum('nij,nik->njk', held_tiles, select(data_rows, row_in), preferr...]
    unnamed x1 -> x0, blocking collectives: 29.1 us -> none
  transfers between devices with their start and end apart: 9 -> 1, of which waited for: 9 -> 1; matrix products, arithmetic and copies ran while one was open for 2% -> 4% of each run, Pallas kernels for 0% -> 0%
where the time goes in v1:
time: 175 us; the launch traced here: 174 us
  Pallas kernels  109 us (62%)
  waiting for transfers between devices  41.8 us (24%)
  local copies, waits for them, and re-layouts  8.42 us (5%)
  other arithmetic  8.09 us (5%)
  starting transfers between devices  6.45 us (4%)
    pallas_call x1, Pallas kernels, shards(): pl.pallas_call(functools.partial(kernel, sizes), out_shape=jax.ShapeDtype...  109 us
    all_to_all x1, waiting for transfers between devices, shards(): lax.all_to_all(slot_tiles, 'rcv', split_axis=0, concat_axis=0, tiled=True)  41.8 us
    all_to_all x1, starting transfers between devices, shards(): lax.all_to_all(slot_tiles, 'rcv', split_axis=0, concat_axis=0, tiled=True)  6.45 us
  transfers between devices with their start and end apart: 1, of which 1 were waited for; matrix products, arithmetic and copies ran while one was open for 4% of the time, Pallas kernels for 0%

profile of v1, /device:TPU:0, one launch (start us, length us, event | category | flops | bytes accessed | tf_op | source)
XLA Modules:
  0.0 174.2 jit_solution(974857996386929072)
XLA Ops:
  0.0 0.9 reduce_window_sum.11
  0.9 0.7 sub.71
  1.6 0.9 dynamic-slice_reduce_fusion.1
  2.5 0.2 dynamic-slice_reduce_fusion
  2.7 0.7 fusion.16
  3.7 0.1 lt.265
  3.8 0.1 lt.273
  4.0 0.1 and.134
  4.2 0.1 fusion.3
  4.4 1.0 gather_fusion.1
  5.4 1.6 broadcast_select_fusion
  7.0 6.4 %all-to-all-start = ((bf16[64,128,128]{2,1,0:T(8,128)(2,1)}), bf16[64,128,128]{2,1,0:T(8,128)(2,1)S(1)}, u32[]{:S(2)}, u32[]{:S(2)}) async-start(bf16[64,128,128]{2,1,0:T(8,128)(2,1)} %broadcast_select_fusion), calls=%async_computation | async-start | bytes 4194304 | tf_op jit(solution)/shard_map/all_to_all | solution.py:416
  13.4 0.1 and.146
  13.5 0.1 add.201
  13.6 0.1 fusion.2
  13.8 0.1 copy.21
  13.9 2.7 %convert_element_type.37.model_half = bf16[32,128,128]{2,1,0:T(8,128)(2,1)} convert(f32[32,128,128]{2,1,0:T(8,128)} %bitcast.13) | non-fusion elementwise | flops 524288 | bytes 3145728 | tf_op jit(solution)/shard_map/convert_element_type | solution.py:480
  16.6 0.6 gather_fusion
  17.3 0.3 select_reduce_fusion.3
  17.6 0.2 convert_reduce_fusion
  17.8 0.2 select_reduce_fusion
  18.1 0.2 convert_reduce_fusion.1
  18.3 0.2 select_reduce_fusion.4
  18.6 0.1 convert_reduce_fusion.4
  18.7 0.1 convert_reduce_fusion.2
  18.8 1.0 constant_dynamic-slice_fusion.model_share
  19.8 41.8 %all-to-all-done.tiles = bf16[64,128,128]{2,1,0:T(8,128)(2,1)S(1)} async-done(((bf16[64,128,128]{2,1,0:T(8,128)(2,1)}), bf16[64,128,128]{2,1,0:T(8,128)(2,1)S(1)}, u32[]{:S(2)}, u32[]{:S(2)}) %all-to-all-start) | async-done | bytes 2097184 | tf_op jit(solution)/shard_map/all_to_all | solution.py:416
  61.6 0.3 broadcast_in_dim.122.weights
  62.0 1.2 copy-done.1
  63.2 1.0 copy-done.2
  64.2 109.2 %shard_map.64 = f32[4,128,128]{2,1,0:T(8,128)S(1)} custom-call(s32[64]{0:T(128)S(1)} %get-tuple-element.19.f_tile, s32[64]{0:T(128)S(1)} %get-tuple-element.18.f_src, f32[64]{0:T(128)S(1)} %fusion.14.f_keep, s32[16]{0:T(128)S(1)} %add_maximum_fusion.1.f_last, f32[16]{0:T(128)S(1)} %compare_convert_fusion.1.f_has, s32[64]{0:T(128)S(1)} %get-tuple-element.14.a_tile, ...), custom_call_target="tpu_custom_call" | custom-call | tf_op jit(solution)/shard_map/pallas_call | solution.py:467
  173.5 0.7 copy.29
  (32 shorter events, 1.0 us)
Async XLA Ops:
  0.0 4.4 %copy-start = (bf16[32,1,1,128,128]{4,3,2,1,0:T(8,128)(2,1)S(1)}, bf16[32,1,1,128,128]{4,3,2,1,0:T(8,128)(2,1)}, u32[]{:S(2)}) copy-start(bf16[32,1,1,128,128]{4,3,2,1,0:T(8,128)(2,1)} %param.6) | copy-start | bytes 3145732
  7.0 6.8 %copy-start.4 = (s32[128,1,1,3]{0,2,3,1:T(1,128)S(1)}, s32[128,1,1,3]{0,2,3,1:T(1,128)}, u32[]{:S(2)}) copy-start(s32[128,1,1,3]{0,2,3,1:T(1,128)} %param.7) | copy-start | bytes 4612
  7.0 54.6 %all-to-all-start = ((bf16[64,128,128]{2,1,0:T(8,128)(2,1)}), bf16[64,128,128]{2,1,0:T(8,128)(2,1)S(1)}, u32[]{:S(2)}, u32[]{:S(2)}) async-start(bf16[64,128,128]{2,1,0:T(8,128)(2,1)} %broadcast_select_fusion), calls=%async_computation | async-start | bytes 4194304 | tf_op jit(solution)/shard_map/all_to_all | solution.py:416
  13.4 3.2 %copy-start.3 = (f32[4,512]{1,0:T(4,128)S(1)}, f32[4,512]{1,0:T(4,128)}, u32[]{:S(2)}) copy-start(f32[4,512]{1,0:T(4,128)} %param.10) | copy-start | bytes 24580
  61.9 1.2 copy-start.1
  63.2 1.0 copy-start.2

commit v2 on v1

--- a/solution.py
+++ b/solution.py
@@ -28,13 +28,13 @@
 
 def kernel(
     sizes,
-    f_tile, f_src, f_keep, f_last, f_has, a_tile, a_row, a_keep, a_last, a_has,
-    tiles, model_half, model_share, observed, weights,
+    routed, f_tile, f_src, f_keep, f_last, f_has, a_tile, a_row, a_keep, a_last, a_has,
+    mine_tiles, model, observed, weight_rows,
     out,
-    prod, psq, own, robust, data, xsend, xrecv, ksend, krecv, zsend, zrecv,
+    tsend, tiles, model_half, weights, prod, psq, own, robust, data, xsend, xrecv, ksend, krecv, zsend, zrecv,
     dksend, dkrecv, dzsend, dzrecv, gsend, gfull, d0, e0, precond, vec, vrecv,
     xs_sem, xr_sem, ks_sem, kr_sem, zs_sem, zr_sem, dks_sem, dkr_sem, dzs_sem, dzr_sem,
-    gs_sem, gr_sem, hs_sem, hr_sem, vs_sem, vr_sem,
+    gs_sem, gr_sem, hs_sem, hr_sem, vs_sem, vr_sem, ts_sem, tr_sem,
 ):
     R, S, T, slots, rows, blocks, bs = sizes
     r, j, k = lax.axis_index("rcv"), lax.axis_index("src"), lax.axis_index("tw")
@@ -243,6 +243,47 @@
         for i in range(R):
             hc(i, sib).wait_recv()
 
+    cap = slots // R
+
+    def tcopy(i, home):
+        return remote(
+            tsend.at[i - 1], tiles.at[pl.ds(home * cap, cap)],
+            ts_sem.at[i - 1], tr_sem.at[i - 1], "rcv", lax.rem(r + i, R),
+        )
+
+    for i in range(1, R):
+        owner = lax.rem(r + i, R)
+
+        def pick(c, _):
+            tsend[i - 1, c] = mine_tiles[routed[owner * cap + c]]
+            return _
+
+        lax.fori_loop(0, cap, pick, 0)
+        copy = tcopy(i, r)
+        copy.start()
+        drain.append(copy)
+
+    def keep_own(c, _):
+        tiles[r * cap + c] = mine_tiles[routed[r * cap + c]]
+        return _
+
+    lax.fori_loop(0, cap, keep_own, 0)
+
+    def cast(b, _):
+        model_half[b] = model[b].astype(BF16)
+        return _
+
+    lax.fori_loop(0, blocks, cast, 0)
+
+    def widen(row, _):
+        line = weight_rows[pl.ds(row, 1), :]
+        weights[row] = jnp.broadcast_to(line, weights.shape[1:]).T
+        return _
+
+    lax.fori_loop(0, rows, widen, 0)
+    for i in range(1, R):
+        tcopy(i, lax.rem(r + R - i, R)).wait_recv()
+
     forward(lambda s: model_half[s])
 
     def first(row, predicted):
@@ -256,7 +297,7 @@
     grad = scatter(0)
     inner0 = jnp.zeros((1, out.shape[2]), F32)
     for b in range(bs):
-        residual = grad[b] - damping * model_share[b]
+        residual = grad[b] - damping * model[(r * T + k) * bs + b]
         scaled = residual / precond[b]
         inner0 = inner0 + jnp.sum(residual * scaled, axis=0, keepdims=True)
         d0[b] = scaled
@@ -349,24 +390,111 @@
         copy.wait_send()
 
 
-def listing_of(key, other, groups):
-    slots = key.shape[0]
-    ids = jnp.arange(slots, dtype=jnp.int32)
-    before = (key[None, :] < key[:, None]) | (
-        (key[None, :] == key[:, None]) & (ids[None, :] < ids[:, None])
-    )
-    rank = jnp.sum(before.astype(jnp.int32), axis=1)
-    hit = rank[None, :] == ids[:, None]
-    order = jnp.sum(jnp.where(hit, ids[None, :], 0), axis=1)
-    partner = jnp.sum(jnp.where(hit, other[None, :], 0), axis=1)
-    sorted_key = jnp.sum(jnp.where(hit, key[None, :], 0), axis=1)
-    keep = jnp.concatenate(
-        [jnp.zeros((1,), F32), (sorted_key[1:] == sorted_key[:-1]).astype(F32)]
-    )
-    group_ids = jnp.arange(groups, dtype=jnp.int32)
-    upto = jnp.sum((key[None, :] <= group_ids[:, None]).astype(jnp.int32), axis=1)
-    count = jnp.sum((key[None, :] == group_ids[:, None]).astype(jnp.int32), axis=1)
-    return order, partner, keep, jnp.maximum(upto - 1, 0), (count > 0).astype(F32)
+def lists_kernel(
+    sizes, counts, listing,
+    routed, f_tile, f_src, f_keep, f_last, f_has, a_tile, a_row, a_keep, a_last, a_has,
+    row_of, block_of, row_next, block_next,
+):
+    R, S, T, slots, rows, blocks, gauges_dev, blocks_col, tiles_dev = sizes
+    r, j, k = lax.axis_index("rcv"), lax.axis_index("src"), lax.axis_index("tw")
+    cap = slots // R
+
+    def clear(n, _):
+        row_next[n] = 0
+        return _
+
+    def clear_block(n, _):
+        block_next[n] = 0
+        return _
+
+    lax.fori_loop(0, rows + 1, clear, 0)
+    lax.fori_loop(0, blocks + 1, clear_block, 0)
+
+    def out_owner(o, start):
+        def one(c, _):
+            routed[o * cap + c] = jnp.minimum(start + c, tiles_dev - 1)
+            return _
+
+        lax.fori_loop(0, cap, one, 0, unroll=True)
+        return start + counts[r, o]
+
+    lax.fori_loop(0, R, out_owner, 0)
+
+    def holder(h, _):
+        start = lax.fori_loop(0, r, lambda o, total: total + counts[h, o], 0)
+        count = counts[h, r]
+
+        def one(c, _):
+            local = start + c
+            place = h * tiles_dev + jnp.minimum(local, tiles_dev - 1)
+            gauge = listing[0, place] - r * gauges_dev
+            valid = (c < count) & (local < tiles_dev) & (gauge >= 0) & (gauge < gauges_dev)
+            row = jnp.where(valid, gauge * blocks_col + listing[2, place] - k * blocks_col, rows)
+            block = jnp.where(valid, listing[1, place] - j * blocks, blocks)
+            slot = h * cap + c
+            row_of[slot] = row
+            block_of[slot] = block
+            row_next[row] = row_next[row] + 1
+            block_next[block] = block_next[block] + 1
+            return _
+
+        return lax.fori_loop(0, cap, one, _, unroll=True)
+
+    lax.fori_loop(0, R, holder, 0)
+
+    def offsets(table, last, has, groups):
+        def one(n, start):
+            count = table[n]
+            table[n] = start
+            last[n] = jnp.maximum(start + count - 1, 0)
+            has[n] = jnp.where(count > 0, 1.0, 0.0).astype(F32)
+            return start + count
+
+        total = lax.fori_loop(0, groups, one, 0)
+        table[groups] = total
+
+    offsets(row_next, f_last, f_has, rows)
+    offsets(block_next, a_last, a_has, blocks)
+
+    def clear_keep(n, _):
+        f_keep[n] = jnp.float32(1.0)
+        a_keep[n] = jnp.float32(1.0)
+        return _
+
+    lax.fori_loop(0, slots, clear_keep, 0, unroll=8)
+
+    def first_row(n, _):
+        f_keep[jnp.minimum(row_next[n], slots - 1)] = jnp.float32(0.0)
+        return _
+
+    def first_block(n, _):
+        a_keep[jnp.minimum(block_next[n], slots - 1)] = jnp.float32(0.0)
+        return _
+
+    def place_one(slot, _):
+        row = row_of[slot]
+        block = block_of[slot]
+        at = row_next[row]
+        row_next[row] = at + 1
+        f_tile[at] = slot
+        f_src[at] = jnp.minimum(block, blocks - 1)
+        at = block_next[block]
+        block_next[block] = at + 1
+        a_tile[at] = slot
+        a_row[at] = jnp.minimum(row, rows - 1)
+        return _
+
+    def mark_row(n, _):
+        pl.when(f_has[n] > 0.0)(lambda: first_row(n, None))
+        return _
+
+    def mark_block(n, _):
+        pl.when(a_has[n] > 0.0)(lambda: first_block(n, None))
+        return _
+
+    lax.fori_loop(0, rows, mark_row, 0)
+    lax.fori_loop(0, blocks, mark_block, 0)
+    lax.fori_loop(0, slots, place_one, 0, unroll=8)
 
 
 def shards(green_tiles, arrivals, counts, observed, weights, source_model):
@@ -378,8 +506,6 @@
     owners = lax.axis_size("rcv")
     columns = lax.axis_size("tw")
     sources = lax.axis_size("src")
-    counts_all = counts.reshape(owners, owners)
-    starts = jnp.cumsum(counts_all, axis=1) - counts_all
     gauges_dev, samples_dev, members = observed.shape
     blocks_col = samples_dev // tile_rows
     rows_dev = gauges_dev * blocks_col
@@ -387,43 +513,8 @@
     blocks_src = src_dev // block_src
     capacity = 2 * tiles_dev // owners
     slots = capacity * owners
-    owner_index = lax.axis_index("rcv")
-    source_index = lax.axis_index("src")
-    column_index = lax.axis_index("tw")
-    slot_ids = jnp.arange(capacity, dtype=jnp.int32)
-    holder_ids = jnp.arange(owners, dtype=jnp.int32)
-    count_in = lax.dynamic_slice_in_dim(counts_all, owner_index, 1, 1)[:, 0]
-    start_in = lax.dynamic_slice_in_dim(starts, owner_index, 1, 1)[:, 0]
-    local_in = start_in[:, None] + slot_ids[None, :]
-    valid_in = (slot_ids[None, :] < count_in[:, None]) & (local_in < tiles_dev)
-    index_in = jnp.where(valid_in, holder_ids[:, None] * tiles_dev + local_in, 0).reshape(-1)
-    listed_in = jnp.take(listing, index_in, axis=0)
-    valid_in = valid_in.reshape(-1) & (listed_in[:, 0] // gauges_dev == owner_index)
-    row_in = jnp.where(
-        valid_in,
-        (listed_in[:, 0] - owner_index * gauges_dev) * blocks_col
-        + listed_in[:, 2]
-        - column_index * blocks_col,
-        rows_dev,
-    )
-    block_in = jnp.where(valid_in, listed_in[:, 1] - source_index * blocks_src, blocks_src)
-    count_out = lax.dynamic_slice_in_dim(counts_all, owner_index, 1, 0)[0]
-    start_out = lax.dynamic_slice_in_dim(starts, owner_index, 1, 0)[0]
-    local_out = start_out[:, None] + slot_ids[None, :]
-    valid_out = (slot_ids[None, :] < count_out[:, None]) & (local_out < tiles_dev)
-    index_out = jnp.where(valid_out, local_out, 0).reshape(-1)
-    slot_tiles = jnp.take(own_tiles, index_out, axis=0)
-    held_tiles = lax.all_to_all(slot_tiles, "rcv", split_axis=0, concat_axis=0, tiled=True)
-    by_row = listing_of(row_in, jnp.minimum(block_in, blocks_src - 1), rows_dev)
-    by_block = listing_of(block_in, jnp.minimum(row_in, rows_dev - 1), blocks_src)
-
     share = blocks_src // (owners * columns)
-    share_index = owner_index * columns + column_index
     model_blocks = source_model.reshape(blocks_src, block_src, members)
-    model_share = lax.dynamic_slice_in_dim(model_blocks, share_index * share, share, 0)
-    weight_wide = jnp.broadcast_to(
-        weights.reshape(rows_dev, tile_rows, 1), (rows_dev, tile_rows, members)
-    )
     sizes = (owners, sources, columns, slots, rows_dev, blocks_src, share)
     full = (block_src, members)
     eight = (8, block_src)
@@ -431,6 +522,10 @@
     stages = columns + owners + sources - 3
     dma = pltpu.SemaphoreType.DMA
     scratch = [
+        pltpu.VMEM((owners - 1, capacity) + full, BF16),
+        pltpu.VMEM((slots,) + full, BF16),
+        pltpu.VMEM((blocks_src,) + full, BF16),
+        pltpu.VMEM((rows_dev,) + full, F32),
         pltpu.VMEM((slots,) + full, F32),
         pltpu.VMEM((slots,) + eight, F32),
         pltpu.VMEM((rows_dev,) + full, F32),
@@ -461,26 +556,45 @@
         dma((2, owners)), dma((2, owners)),
         dma((2, owners)), dma((2, owners)),
         dma((stages,)), dma((stages,)),
+        dma((owners - 1,)), dma((owners - 1,)),
     ]
     vmem = pl.BlockSpec(memory_space=pltpu.VMEM)
     smem = pl.BlockSpec(memory_space=pltpu.SMEM)
+    ints, floats = (lambda n: jax.ShapeDtypeStruct((n,), jnp.int32)), (
+        lambda n: jax.ShapeDtypeStruct((n,), F32)
+    )
+    table = (sizes[:6]) + (gauges_dev, blocks_col, tiles_dev)
+    lists = pl.pallas_call(
+        functools.partial(lists_kernel, table),
+        out_shape=(
+            ints(slots),
+            ints(slots), ints(slots), floats(slots), ints(rows_dev), floats(rows_dev),
+            ints(slots), ints(slots), floats(slots), ints(blocks_src), floats(blocks_src),
+        ),
+        in_specs=[smem] * 2,
+        out_specs=(smem,) * 11,
+        scratch_shapes=[
+            pltpu.SMEM((slots,), jnp.int32),
+            pltpu.SMEM((slots,), jnp.int32),
+            pltpu.SMEM((rows_dev + 1,), jnp.int32),
+            pltpu.SMEM((blocks_src + 1,), jnp.int32),
+        ],
+    )(counts.reshape(owners, owners), listing.T)
     update = pl.pallas_call(
         functools.partial(kernel, sizes),
         out_shape=jax.ShapeDtypeStruct((share,) + full, F32),
-        in_specs=[smem] * 10 + [vmem] * 5,
+        in_specs=[smem] * 11 + [vmem] * 4,
         out_specs=vmem,
         scratch_shapes=scratch,
         compiler_params=pltpu.CompilerParams(
             collective_id=0, has_side_effects=True, vmem_limit_bytes=48 * 1024 * 1024
         ),
     )(
-        *by_row,
-        *by_block,
-        held_tiles,
-        model_blocks.astype(BF16),
-        model_share,
+        *lists,
+        own_tiles,
+        model_blocks,
         observed.reshape(rows_dev, tile_rows, members),
-        weight_wide,
+        weights.reshape(rows_dev, tile_rows),
     )
     return update.reshape(1, share * block_src, members)
 

time: 175 us -> 174 us (level)
  Pallas kernels: 109 us -> 160 us
  waiting for transfers between devices: 41.8 us -> 0 us
  other arithmetic: 8.09 us -> 0 us
  starting transfers between devices: 6.45 us -> 0 us
  local copies, waits for them, and re-layouts: 8.42 us -> 13.5 us
    pallas_call x1, Pallas kernels: 109 us -> 156 us  [shards(): pl.pallas_call(functools.partial(kernel, sizes), out_shape=jax.ShapeDtype...]
    all_to_all x1 -> x0, waiting for transfers between devices: 41.8 us -> none  [shards(): lax.all_to_all(slot_tiles, 'rcv', split_axis=0, concat_axis=0, tiled=True)]
    unnamed x12 -> x30, local copies, waits for them, and re-layouts: 3.09 us -> 12.8 us
    all_to_all x1 -> x0, starting transfers between devices: 6.45 us -> none  [shards(): lax.all_to_all(slot_tiles, 'rcv', split_axis=0, concat_axis=0, tiled=True)]
    pallas_call x0 -> x1, Pallas kernels: none -> 4.05 us  [shards(): pl.pallas_call(functools.partial(lists_kernel, table), out_shape=(ints(sl...]
    convert_element_type x3 -> x0, other arithmetic: 2.75 us -> none  [the longest x1 2.74 us: shards(): model_blocks.astype(BF16)]
    select_n x5 -> x0, other arithmetic: 2.17 us -> none  [the longest x2 1.72 us: shards(): slot_tiles = jnp.take(own_tiles, index_out, axis=0)]
    dynamic_slice x3 -> x0, local copies, waits for them, and re-layouts: 2.07 us -> none  [the longest x1 0.98 us: shards(): lax.dynamic_slice_in_dim(model_blocks, share_index * share, share, 0)]
  transfers between devices with their start and end apart: 1 -> 0, of which waited for: 1 -> 0; matrix products, arithmetic and copies ran while one was open for 4% -> 0% of each run, Pallas kernels for 0% -> 0%
where the time goes in v2:
time: 174 us; the launch traced here: 173 us
  Pallas kernels  160 us (92%)
  local copies, waits for them, and re-layouts  13.5 us (8%)
    pallas_call x1, Pallas kernels, shards(): pl.pallas_call(functools.partial(kernel, sizes), out_shape=jax.ShapeDtype...  156 us
    unnamed x30, local copies, waits for them, and re-layouts  12.8 us
    pallas_call x1, Pallas kernels, shards(): pl.pallas_call(functools.partial(lists_kernel, table), out_shape=(ints(sl...  4.05 us

profile of v2, /device:TPU:0, one launch (start us, length us, event | category | flops | bytes accessed | tf_op | source)
XLA Modules:
  0.0 173.1 jit_solution(6053165499920240652)
XLA Ops:
  0.0 1.3 copy.9
  1.3 4.1 %shard_map.64 = (s32[64]{0:T(128)}, s32[64]{0:T(128)}, s32[64]{0:T(128)}, f32[64]{0:T(128)}, s32[16]{0:T(128)}, /*index=5*/f32[16]{0:T(128)}, s32[64]{0:T(128)},...) custom-call(s32[4,4]{1,0:T(4,128)} %bitcast.15, s32[3,128]{1,0:T(4,128)} %bitcast.14), custom_call_target="tpu_custom_call" | custom-call | tf_op jit(solution)/shard_map/pallas_call | solution.py:567
  5.3 0.7 reshape.26.weight_rows
  6.0 0.0 copy-start
  6.0 1.6 copy-done
  7.6 0.0 copy-start.1
  7.6 1.2 copy-done.1
  8.8 0.0 copy-start.2
  8.8 1.0 copy-done.2
  9.9 0.0 copy-start.3
  9.9 0.6 copy-done.3
  10.5 0.0 copy-start.4
  10.5 0.7 copy-done.4
  11.2 0.0 copy-start.5
  11.2 0.6 copy-done.5
  11.8 0.0 copy-start.6
  11.8 0.6 copy-done.6
  12.4 0.0 copy-start.7
  12.4 0.7 copy-done.7
  13.1 0.0 copy-start.8
  13.1 0.7 copy-done.8
  13.7 0.0 copy-start.9
  13.7 0.6 copy-done.9
  14.3 0.0 copy-start.10
  14.3 0.6 copy-done.10
  14.9 0.0 copy-start.11
  14.9 0.6 copy-done.11
  15.6 0.7 copy-done.12
  16.3 0.0 copy-start.13
  16.3 0.6 copy-done.13
  16.9 155.5 %shard_map.65 = f32[4,128,128]{2,1,0:T(8,128)S(1)} custom-call(s32[64]{0:T(128)S(1)} %copy-done.3, s32[64]{0:T(128)S(1)} %copy-done.4, s32[64]{0:T(128)S(1)} %copy-done.5, f32[64]{0:T(128)S(1)} %copy-done.6, s32[16]{0:T(128)S(1)} %copy-done.7, f32[16]{0:T(128)S(1)} %copy-done.8, s32[64]{0:T(128)S(1)} %copy-done.9, s32[64]{0:T(128)S(1)} %copy-done.10, ...), custom_call_target="tpu_custom_call" | custom-call | tf_op jit(solution)/shard_map/pallas_call | solution.py:583
  172.4 0.7 copy.11
  (1 shorter events, 0.0 us)
Async XLA Ops:
  6.0 1.6 copy-start
  7.6 1.2 copy-start.1
  8.8 1.0 copy-start.2
  9.9 0.6 copy-start.3
  10.5 0.7 copy-start.4
  11.2 0.6 copy-start.5
  11.8 0.6 copy-start.6
  12.4 0.7 copy-start.7
  13.1 0.7 copy-start.8
  13.7 0.6 copy-start.9
  14.3 0.6 copy-start.10
  14.9 0.6 copy-start.11
  15.6 0.7 copy-start.12
  16.3 0.6 copy-start.13

commit v3 on v2

--- a/solution.py
+++ b/solution.py
@@ -26,21 +26,57 @@
     )
 
 
+class View:
+    def __init__(self, ref, base, real):
+        self.ref, self.base, self.real = ref, base, real
+
+    def __getitem__(self, index):
+        value = self.ref[self.base + index]
+        return value.astype(F32) if self.real else value
+
+    def __setitem__(self, index, value):
+        self.ref[self.base + index] = value
+
+
+def views(ref, slots, rows, blocks, real=True):
+    base = 0
+    result = []
+    for length, flag in (
+        (slots, False),
+        (slots, False), (slots, False), (slots, True), (rows, False), (rows, True),
+        (slots, False), (slots, False), (slots, True), (blocks, False), (blocks, True),
+    ):
+        result.append(View(ref, base, flag and real))
+        base += length
+    return result
+
+
 def kernel(
     sizes,
-    routed, f_tile, f_src, f_keep, f_last, f_has, a_tile, a_row, a_keep, a_last, a_has,
-    mine_tiles, model, observed, weight_rows,
+    packed, tiles_any, model_any, observed_any, weight_rows,
     out,
+    mine_tiles, model, observed, in_sem,
     tsend, tiles, model_half, weights, prod, psq, own, robust, data, xsend, xrecv, ksend, krecv, zsend, zrecv,
     dksend, dkrecv, dzsend, dzrecv, gsend, gfull, d0, e0, precond, vec, vrecv,
     xs_sem, xr_sem, ks_sem, kr_sem, zs_sem, zr_sem, dks_sem, dkr_sem, dzs_sem, dzr_sem,
     gs_sem, gr_sem, hs_sem, hr_sem, vs_sem, vr_sem, ts_sem, tr_sem,
 ):
     R, S, T, slots, rows, blocks, bs = sizes
+    (routed, f_tile, f_src, f_keep, f_last, f_has, a_tile, a_row, a_keep, a_last, a_has) = views(
+        packed, slots, rows, blocks
+    )
     r, j, k = lax.axis_index("rcv"), lax.axis_index("src"), lax.axis_index("tw")
     sib = 1 - k
     per = rows // CHUNKS
     drain = []
+
+    inward = [
+        pltpu.make_async_copy(tiles_any, mine_tiles, in_sem.at[2]),
+        pltpu.make_async_copy(model_any, model, in_sem.at[0]),
+        pltpu.make_async_copy(observed_any, observed, in_sem.at[1]),
+    ]
+    for copy in inward:
+        copy.start()
 
     barrier = pltpu.get_barrier_semaphore()
     pl.semaphore_signal(barrier, inc=1, device_id={"tw": sib}, device_id_type=MESH)
@@ -251,6 +287,7 @@
             ts_sem.at[i - 1], tr_sem.at[i - 1], "rcv", lax.rem(r + i, R),
         )
 
+    inward.pop(0).wait()
     for i in range(1, R):
         owner = lax.rem(r + i, R)
 
@@ -269,18 +306,21 @@
 
     lax.fori_loop(0, cap, keep_own, 0)
 
+    for copy in inward:
+        copy.wait()
+
     def cast(b, _):
         model_half[b] = model[b].astype(BF16)
         return _
 
     lax.fori_loop(0, blocks, cast, 0)
 
-    def widen(row, _):
-        line = weight_rows[pl.ds(row, 1), :]
+    span = weights.shape[1]
+    groups = rows // weight_rows.shape[0]
+    for row in range(rows):
+        g, b = divmod(row, groups)
+        line = weight_rows[g : g + 1, b * span : (b + 1) * span]
         weights[row] = jnp.broadcast_to(line, weights.shape[1:]).T
-        return _
-
-    lax.fori_loop(0, rows, widen, 0)
     for i in range(1, R):
         tcopy(i, lax.rem(r + R - i, R)).wait_recv()
 
@@ -392,10 +432,13 @@
 
 def lists_kernel(
     sizes, counts, listing,
-    routed, f_tile, f_src, f_keep, f_last, f_has, a_tile, a_row, a_keep, a_last, a_has,
+    packed,
     row_of, block_of, row_next, block_next,
 ):
     R, S, T, slots, rows, blocks, gauges_dev, blocks_col, tiles_dev = sizes
+    (routed, f_tile, f_src, f_keep, f_last, f_has, a_tile, a_row, a_keep, a_last, a_has) = views(
+        packed, slots, rows, blocks, real=False
+    )
     r, j, k = lax.axis_index("rcv"), lax.axis_index("src"), lax.axis_index("tw")
     cap = slots // R
 
@@ -427,10 +470,10 @@
         def one(c, _):
             local = start + c
             place = h * tiles_dev + jnp.minimum(local, tiles_dev - 1)
-            gauge = listing[0, place] - r * gauges_dev
+            gauge = listing[0, 0, place] - r * gauges_dev
             valid = (c < count) & (local < tiles_dev) & (gauge >= 0) & (gauge < gauges_dev)
-            row = jnp.where(valid, gauge * blocks_col + listing[2, place] - k * blocks_col, rows)
-            block = jnp.where(valid, listing[1, place] - j * blocks, blocks)
+            row = jnp.where(valid, gauge * blocks_col + listing[2, 0, place] - k * blocks_col, rows)
+            block = jnp.where(valid, listing[1, 0, place] - j * blocks, blocks)
             slot = h * cap + c
             row_of[slot] = row
             block_of[slot] = block
@@ -447,7 +490,7 @@
             count = table[n]
             table[n] = start
             last[n] = jnp.maximum(start + count - 1, 0)
-            has[n] = jnp.where(count > 0, 1.0, 0.0).astype(F32)
+            has[n] = jnp.where(count > 0, 1, 0)
             return start + count
 
         total = lax.fori_loop(0, groups, one, 0)
@@ -457,18 +500,18 @@
     offsets(block_next, a_last, a_has, blocks)
 
     def clear_keep(n, _):
-        f_keep[n] = jnp.float32(1.0)
-        a_keep[n] = jnp.float32(1.0)
+        f_keep[n] = 1
+        a_keep[n] = 1
         return _
 
     lax.fori_loop(0, slots, clear_keep, 0, unroll=8)
 
     def first_row(n, _):
-        f_keep[jnp.minimum(row_next[n], slots - 1)] = jnp.float32(0.0)
+        f_keep[jnp.minimum(row_next[n], slots - 1)] = 0
         return _
 
     def first_block(n, _):
-        a_keep[jnp.minimum(block_next[n], slots - 1)] = jnp.float32(0.0)
+        a_keep[jnp.minimum(block_next[n], slots - 1)] = 0
         return _
 
     def place_one(slot, _):
@@ -485,11 +528,11 @@
         return _
 
     def mark_row(n, _):
-        pl.when(f_has[n] > 0.0)(lambda: first_row(n, None))
+        pl.when(f_has[n] > 0)(lambda: first_row(n, None))
         return _
 
     def mark_block(n, _):
-        pl.when(a_has[n] > 0.0)(lambda: first_block(n, None))
+        pl.when(a_has[n] > 0)(lambda: first_block(n, None))
         return _
 
     lax.fori_loop(0, rows, mark_row, 0)
@@ -502,7 +545,7 @@
         green_tiles.shape[0], green_tiles.shape[3], green_tiles.shape[4]
     )
     tiles_dev, tile_rows, block_src = own_tiles.shape
-    listing = arrivals.reshape(arrivals.shape[0], 3)
+    listing = arrivals.transpose(1, 3, 2, 0).reshape(3, 1, arrivals.shape[0])
     owners = lax.axis_size("rcv")
     columns = lax.axis_size("tw")
     sources = lax.axis_size("src")
@@ -522,6 +565,10 @@
     stages = columns + owners + sources - 3
     dma = pltpu.SemaphoreType.DMA
     scratch = [
+        pltpu.VMEM((tiles_dev,) + full, BF16),
+        pltpu.VMEM((blocks_src,) + full, F32),
+        pltpu.VMEM((rows_dev,) + full, BF16),
+        pltpu.SemaphoreType.DMA((3,)),
         pltpu.VMEM((owners - 1, capacity) + full, BF16),
         pltpu.VMEM((slots,) + full, BF16),
         pltpu.VMEM((blocks_src,) + full, BF16),
@@ -559,42 +606,36 @@
         dma((owners - 1,)), dma((owners - 1,)),
     ]
     vmem = pl.BlockSpec(memory_space=pltpu.VMEM)
+    hbm = pl.BlockSpec(memory_space=pltpu.HBM)
     smem = pl.BlockSpec(memory_space=pltpu.SMEM)
-    ints, floats = (lambda n: jax.ShapeDtypeStruct((n,), jnp.int32)), (
-        lambda n: jax.ShapeDtypeStruct((n,), F32)
-    )
     table = (sizes[:6]) + (gauges_dev, blocks_col, tiles_dev)
     lists = pl.pallas_call(
         functools.partial(lists_kernel, table),
-        out_shape=(
-            ints(slots),
-            ints(slots), ints(slots), floats(slots), ints(rows_dev), floats(rows_dev),
-            ints(slots), ints(slots), floats(slots), ints(blocks_src), floats(blocks_src),
-        ),
+        out_shape=jax.ShapeDtypeStruct((7 * slots + 2 * rows_dev + 2 * blocks_src,), jnp.int32),
         in_specs=[smem] * 2,
-        out_specs=(smem,) * 11,
+        out_specs=smem,
         scratch_shapes=[
             pltpu.SMEM((slots,), jnp.int32),
             pltpu.SMEM((slots,), jnp.int32),
             pltpu.SMEM((rows_dev + 1,), jnp.int32),
             pltpu.SMEM((blocks_src + 1,), jnp.int32),
         ],
-    )(counts.reshape(owners, owners), listing.T)
+    )(counts.reshape(owners, owners), listing)
     update = pl.pallas_call(
         functools.partial(kernel, sizes),
         out_shape=jax.ShapeDtypeStruct((share,) + full, F32),
-        in_specs=[smem] * 11 + [vmem] * 4,
+        in_specs=[smem, hbm, hbm, hbm, vmem],
         out_specs=vmem,
         scratch_shapes=scratch,
         compiler_params=pltpu.CompilerParams(
-            collective_id=0, has_side_effects=True, vmem_limit_bytes=48 * 1024 * 1024
+            collective_id=0, has_side_effects=True, vmem_limit_bytes=63 * 1024 * 1024
         ),
     )(
-        *lists,
+        lists,
         own_tiles,
         model_blocks,
         observed.reshape(rows_dev, tile_rows, members),
-        weights.reshape(rows_dev, tile_rows),
+        weights,
     )
     return update.reshape(1, share * block_src, members)
 

time: 174 us -> 162 us (0.931)
  local copies, waits for them, and re-layouts: 13.5 us -> 1.67 us
    unnamed x30 -> x1, local copies, waits for them, and re-layouts: 12.8 us -> 1.67 us
where the time goes in v3:
time: 162 us
  Pallas kernels  161 us (99%)
  local copies, waits for them, and re-layouts  1.67 us (1%)
    pallas_call x1, Pallas kernels, shards(): pl.pallas_call(functools.partial(kernel, sizes), out_shape=jax.ShapeDtype...  156 us
    pallas_call x1, Pallas kernels, shards(): pl.pallas_call(functools.partial(lists_kernel, table), out_shape=jax.Shap...  4.13 us

profile of v3, /device:TPU:0, one launch (start us, length us, event | category | flops | bytes accessed | tf_op | source)
XLA Modules:
  0.0 162.2 jit_solution(785145273313617134)
XLA Ops:
  0.0 4.1 %shard_map.64.packed = s32[544]{0:T(1024)} custom-call(s32[4,4]{1,0:T(4,128)} %bitcast.12, s32[3,1,128]{2,1,0:T(1,128)} %bitcast.13), custom_call_target="tpu_custom_call" | custom-call | tf_op jit(solution)/shard_map/pallas_call | solution.py:612
  4.1 156.4 %shard_map.65 = f32[4,128,128]{2,1,0:T(8,128)} custom-call(s32[544]{0:T(1024)} %shard_map.64.packed, bf16[32,128,128]{2,1,0:T(8,128)(2,1)} %bitcast.9, f32[32,128,128]{2,1,0:T(8,128)} %bitcast.8, bf16[16,128,128]{2,1,0:T(8,128)(2,1)} %bitcast.11, f32[4,512]{1,0:T(4,128)} %weight_rows.1), custom_call_target="tpu_custom_call" | custom-call | tf_op jit(solution)/shard_map/pallas_call | solution.py:624
  160.6 1.7 %copy.8 = f32[1,512,128]{2,1,0:T(8,128)} copy(f32[1,512,128]{2,1,0:T(8,128)} %bitcast.10) | data formatting | bytes 524288

commit v4 on v3

--- a/solution.py
+++ b/solution.py
@@ -69,6 +69,7 @@
     sib = 1 - k
     per = rows // CHUNKS
     drain = []
+    late = []
 
     inward = [
         pltpu.make_async_copy(tiles_any, mine_tiles, in_sem.at[2]),
@@ -246,38 +247,87 @@
         mine = place(r, k)
         gfull[rnd, mine] = gsend[rnd]
 
-        def zc(i):
-            return remote(
-                gsend.at[rnd], gfull.at[rnd, mine],
-                gs_sem.at[rnd, i], gr_sem.at[rnd, i], "rcv", lax.rem(r + i, R),
-            )
-
-        def zwait(i):
-            spot = place(lax.rem(r + R - i, R), k)
-            remote(
-                gsend.at[rnd], gfull.at[rnd, spot],
-                gs_sem.at[rnd, i], gr_sem.at[rnd, i], "rcv", lax.rem(r + i, R),
-            ).wait_recv()
-
-        def hc(i, core):
-            spot = place(lax.rem(r + R - i, R), core)
+        def hop(way, d):
+            sign = 1 - 2 * way
+            spot = place(lax.rem(r - sign * (d - 1) + R, R), k)
             return remote(
                 gfull.at[rnd, spot], gfull.at[rnd, spot],
-                hs_sem.at[rnd, i], hr_sem.at[rnd, i], "tw", sib,
+                gs_sem.at[rnd, way, d], gr_sem.at[rnd, way, d], "rcv", lax.rem(r + sign + R, R),
             )
 
-        for i in range(1, R):
-            copy = zc(i)
-            copy.start()
-            drain.append(copy)
-        for i in range(R):
-            if i > 0:
-                zwait(i)
-            copy = hc(i, k)
-            copy.start()
-            drain.append(copy)
-        for i in range(R):
-            hc(i, sib).wait_recv()
+        def arrival(way, d):
+            sign = 1 - 2 * way
+            spot = place(lax.rem(r - sign * d + R, R), k)
+            return remote(
+                gfull.at[rnd, spot], gfull.at[rnd, spot],
+                gs_sem.at[rnd, way, d], gr_sem.at[rnd, way, d], "rcv", lax.rem(r + sign + R, R),
+            )
+
+        def side(way, d, core):
+            sign = 1 - 2 * way
+            spot = place(lax.rem(r - sign * d + R, R), core)
+            return remote(
+                gfull.at[rnd, spot], gfull.at[rnd, spot],
+                hs_sem.at[rnd, way, d], hr_sem.at[rnd, way, d], "tw", sib,
+            )
+
+        def come(way, d):
+            return r >= d if way == 0 else r + d < R
+
+        def goes(way, d):
+            if way == 0:
+                return (r >= d - 1) & (r + 1 < R)
+            return (r + d - 1 < R) & (r >= 1)
+
+        for d in range(1, R):
+            for way in range(2):
+                if d > 1:
+
+                    @pl.when(come(way, d - 1))
+                    def _():
+                        arrival(way, d - 1).wait_recv()
+
+                @pl.when(goes(way, d))
+                def _():
+                    hop(way, d).start()
+
+                if d > 1:
+
+                    @pl.when(come(way, d - 1))
+                    def _():
+                        side(way, d - 1, k).start()
+
+            if d == 1:
+                side(0, 0, k).start()
+        for way in range(2):
+
+            @pl.when(come(way, R - 1))
+            def _():
+                arrival(way, R - 1).wait_recv()
+                side(way, R - 1, k).start()
+
+        side(0, 0, sib).wait_recv()
+        for d in range(1, R):
+            for way in range(2):
+
+                @pl.when(come(way, d))
+                def _():
+                    side(way, d, sib).wait_recv()
+
+        def settle():
+            side(0, 0, k).wait_send()
+            for d in range(1, R):
+                for way in range(2):
+
+                    @pl.when(goes(way, d))
+                    def _():
+                        hop(way, d).wait_send()
+
+                    @pl.when(come(way, d))
+                    def _():
+                        side(way, d, k).wait_send()
+
+        late.append(settle)
 
     cap = slots // R
 
@@ -428,6 +478,8 @@
         out[b] = step0 * direction + step1 * (grow * direction - step0 * e0[b])
     for copy in drain:
         copy.wait_send()
+    for settle in late:
+        settle()
 
 
 def lists_kernel(
@@ -600,8 +652,8 @@
         dma((2, owners)), dma((2, owners)),
         dma((1,)), dma((1,)),
         dma((owners,)), dma((owners,)),
-        dma((2, owners)), dma((2, owners)),
-        dma((2, owners)), dma((2, owners)),
+        dma((2, 2, owners)), dma((2, 2, owners)),
+        dma((2, 2, owners)), dma((2, 2, owners)),
         dma((stages,)), dma((stages,)),
         dma((owners - 1,)), dma((owners - 1,)),
     ]

time: 162 us -> 160 us (0.988)
  Pallas kernels: 161 us -> 158 us
    pallas_call x1, Pallas kernels: 156 us -> 154 us  [shards(): pl.pallas_call(functools.partial(kernel, sizes), out_shape=jax.ShapeDtype...]
where the time goes in v4:
time: 160 us
  Pallas kernels  158 us (99%)
  local copies, waits for them, and re-layouts  1.67 us (1%)
    pallas_call x1, Pallas kernels, shards(): pl.pallas_call(functools.partial(kernel, sizes), out_shape=jax.ShapeDtype...  154 us
    pallas_call x1, Pallas kernels, shards(): pl.pallas_call(functools.partial(lists_kernel, table), out_shape=jax.Shap...  4.13 us

profile of v4, /device:TPU:0, one launch (start us, length us, event | category | flops | bytes accessed | tf_op | source)
XLA Modules:
  0.0 160.0 jit_solution(11294294280237248796)
XLA Ops:
  0.0 4.1 %shard_map.64.packed = s32[544]{0:T(1024)} custom-call(s32[4,4]{1,0:T(4,128)} %bitcast.12, s32[3,1,128]{2,1,0:T(1,128)} %bitcast.13), custom_call_target="tpu_custom_call" | custom-call | tf_op jit(solution)/shard_map/pallas_call | solution.py:664
  4.1 154.1 %shard_map.65 = f32[4,128,128]{2,1,0:T(8,128)} custom-call(s32[544]{0:T(1024)} %shard_map.64.packed, bf16[32,128,128]{2,1,0:T(8,128)(2,1)} %bitcast.9, f32[32,128,128]{2,1,0:T(8,128)} %bitcast.8, bf16[16,128,128]{2,1,0:T(8,128)(2,1)} %bitcast.11, f32[4,512]{1,0:T(4,128)} %weight_rows.1), custom_call_target="tpu_custom_call" | custom-call | tf_op jit(solution)/shard_map/pallas_call | solution.py:676
  158.3 1.7 %copy.8 = f32[1,512,128]{2,1,0:T(8,128)} copy(f32[1,512,128]{2,1,0:T(8,128)} %bitcast.10) | data formatting | bytes 524288

commit v5 on v4

--- a/solution.py
+++ b/solution.py
@@ -70,6 +70,7 @@
     per = rows // CHUNKS
     drain = []
     late = []
+    far = sorted(range(1, R), key=lambda i: -min(i, R - i))
 
     inward = [
         pltpu.make_async_copy(tiles_any, mine_tiles, in_sem.at[2]),
@@ -176,7 +177,7 @@
             dzsend.at[i], dzrecv.at[i], dzs_sem.at[i], dzr_sem.at[i], "rcv", lax.rem(r + i, R)
         )
 
-    order = list(range(1, R)) + [0]
+    order = far + [0]
 
     def scatter(rnd):
         for i in order:
@@ -338,14 +339,14 @@
         )
 
     inward.pop(0).wait()
-    for i in range(1, R):
+    for i in far:
         owner = lax.rem(r + i, R)
 
         def pick(c, _):
             tsend[i - 1, c] = mine_tiles[routed[owner * cap + c]]
             return _
 
-        lax.fori_loop(0, cap, pick, 0)
+        lax.fori_loop(0, cap, pick, 0, unroll=4)
         copy = tcopy(i, r)
         copy.start()
         drain.append(copy)
@@ -502,8 +503,8 @@
         block_next[n] = 0
         return _
 
-    lax.fori_loop(0, rows + 1, clear, 0)
-    lax.fori_loop(0, blocks + 1, clear_block, 0)
+    lax.fori_loop(0, rows + 1, clear, 0, unroll=True)
+    lax.fori_loop(0, blocks + 1, clear_block, 0, unroll=True)
 
     def out_owner(o, start):
         def one(c, _):
@@ -545,7 +546,7 @@
             has[n] = jnp.where(count > 0, 1, 0)
             return start + count
 
-        total = lax.fori_loop(0, groups, one, 0)
+        total = lax.fori_loop(0, groups, one, 0, unroll=8)
         table[groups] = total
 
     offsets(row_next, f_last, f_has, rows)
@@ -587,8 +588,8 @@
         pl.when(a_has[n] > 0)(lambda: first_block(n, None))
         return _
 
-    lax.fori_loop(0, rows, mark_row, 0)
-    lax.fori_loop(0, blocks, mark_block, 0)
+    lax.fori_loop(0, rows, mark_row, 0, unroll=8)
+    lax.fori_loop(0, blocks, mark_block, 0, unroll=8)
     lax.fori_loop(0, slots, place_one, 0, unroll=8)
 
 

time: 160 us -> 156 us (0.975)
  Pallas kernels: 158 us -> 154 us
    pallas_call x1, Pallas kernels: 154 us -> 151 us  [shards(): pl.pallas_call(functools.partial(kernel, sizes), out_shape=jax.ShapeDtype...]
where the time goes in v5:
time: 156 us
  Pallas kernels  154 us (99%)
  local copies, waits for them, and re-layouts  1.67 us (1%)
    pallas_call x1, Pallas kernels, shards(): pl.pallas_call(functools.partial(kernel, sizes), out_shape=jax.ShapeDtype...  151 us
    pallas_call x1, Pallas kernels, shards(): pl.pallas_call(functools.partial(lists_kernel, table), out_shape=jax.Shap...  3.6 us

profile of v5, /device:TPU:0, one launch (start us, length us, event | category | flops | bytes accessed | tf_op | source)
XLA Modules:
  0.0 156.0 jit_solution(17361988273262143205)
XLA Ops:
  0.0 3.6 %shard_map.64.packed = s32[544]{0:T(1024)} custom-call(s32[4,4]{1,0:T(4,128)} %bitcast.12, s32[3,1,128]{2,1,0:T(1,128)} %bitcast.13), custom_call_target="tpu_custom_call" | custom-call | tf_op jit(solution)/shard_map/pallas_call | solution.py:665
  3.6 150.7 %shard_map.65 = f32[4,128,128]{2,1,0:T(8,128)} custom-call(s32[544]{0:T(1024)} %shard_map.64.packed, bf16[32,128,128]{2,1,0:T(8,128)(2,1)} %bitcast.9, f32[32,128,128]{2,1,0:T(8,128)} %bitcast.8, bf16[16,128,128]{2,1,0:T(8,128)(2,1)} %bitcast.11, f32[4,512]{1,0:T(4,128)} %weight_rows.1), custom_call_target="tpu_custom_call" | custom-call | tf_op jit(solution)/shard_map/pallas_call | solution.py:677
  154.3 1.7 %copy.8 = f32[1,512,128]{2,1,0:T(8,128)} copy(f32[1,512,128]{2,1,0:T(8,128)} %bitcast.10) | data formatting | bytes 524288
